TPU v7x, 32 devices: a whole 2x2x4 slice. The times are simulated.
32 devices in a mesh: ka: 2 (over core), slab: 16 (over z, y, x).
Axes of the slice: x: 2, y: 2, z: 4, core: 2. Of those that a mesh axis runs over, the one named last changes fastest.
Arguments:
- packet_prev: float32 [2, 128, 256, 384], P('ka', 'slab'), may hold values from -18 to 18
- packet_now: float32 [2, 128, 256, 384], P('ka', 'slab'), may hold values from -18 to 18
- potential: float32 [128, 256, 384], P('slab'), may hold values from 0.05 to 0.5
- kin_rho: float32 [128, 128], replicated, may hold values from -1 to 1, as said below
- kin_theta: float32 [256, 256], replicated, may hold values from -1 to 1, as said below
- kin_phi: float32 [384, 384], replicated, may hold values from -1 to 1, as said below
- damping: float32 [128], P('slab'), may hold values from 0.8 to 1
- inertia: float32 [128], P('slab'), may hold values from 0.05 to 0.3
- tilt: float32 [256], replicated, may hold values from 0.5 to 2
Outputs:
- packet_last: float32 [2, 128, 256, 384], P('ka', 'slab')
- packet_before: float32 [2, 128, 256, 384], P('ka', 'slab')
- intersections: float32 [2, 2], P(None, 'ka')
Inputs may be any that keep to these rules, and one draw needn't show every extreme that they name: `kin_rho`: symmetric. `kin_theta`: symmetric. `kin_phi`: symmetric.
All inputs are finite; a program needn't handle non-finite values.
Results may differ from a plain program's by a relative error of at most 0.0001.
Values sent between devices are 32-bit elements; how exact they have to be, the bound alone decides.
A program may use at most 128 MiB of HBM per device.

v0:
```python
import jax
import jax.numpy as jnp
from jax import lax
from jax.sharding import PartitionSpec as P

NR = 128
NT = 256
NP = 384
STEPS = 2
JTOT = 60
K_FIRST = 0
HI = lax.Precision.HIGHEST


def padded(cells, sides, width):
    for axis, dim in sides:
        count = lax.axis_size(axis)
        ends = count - 1
        head = lax.slice_in_dim(cells, 0, width, axis=dim)
        tail = lax.slice_in_dim(cells, cells.shape[dim] - width, cells.shape[dim], axis=dim)
        cells = jnp.concatenate(
            [
                lax.ppermute(tail, axis, [(i, (i + 1) % count) for i in range(ends)]),
                cells,
                lax.ppermute(head, axis, [((i + 1) % count, i) for i in range(ends)]),
            ],
            axis=dim,
        )
    return cells


def rho_apply(kin_rho, whole):
    return jnp.einsum("sr,rtp->stp", kin_rho, whole, precision=HI)


def apply_h(q, potential, kin_rho, kin_theta, kin_phi, inertia, tilt):
    kval = (K_FIRST + lax.axis_index("ka")).astype(jnp.float32)
    jj = float(JTOT * (JTOT + 1))
    cent = (jj - 2.0 * kval * kval) / float(JTOT * JTOT)
    lam_here = jnp.sqrt(jj - kval * (kval + 1.0)) / float(JTOT)
    lam_below = jnp.sqrt(jj - (kval - 1.0) * kval) / float(JTOT)
    near = padded(q, (("ka", 0),), 1)
    field = q[0]
    term = rho_apply(
        kin_rho, lax.all_to_all(field, "slab", split_axis=1, concat_axis=0, tiled=True)
    )
    rho_part = lax.all_to_all(term, "slab", split_axis=0, concat_axis=1, tiled=True)
    theta_part = jnp.einsum("ts,rsp->rtp", kin_theta, field, precision=HI)
    rows = field.shape[0] * field.shape[1]
    phi_part = jnp.dot(field.reshape(rows, field.shape[2]), kin_phi, precision=HI).reshape(
        field.shape
    )
    coupling = (
        inertia[:, None, None] * tilt[None, :, None] * (lam_here * near[2] + lam_below * near[0])
    )
    diag = potential + inertia[:, None, None] * cent
    total = rho_part + theta_part + phi_part + diag * field + coupling
    return total[None]


def shards(packet_prev, packet_now, potential, kin_rho, kin_theta, kin_phi, damping, inertia, tilt):
    damp = damping[None, :, None, None]
    cells = float(NR * NT * NP)
    q_prev = packet_prev
    q = packet_now
    partials = []
    for step in range(STEPS):
        image = apply_h(q, potential, kin_rho, kin_theta, kin_phi, inertia, tilt)
        q_new = damp * (2.0 * image - damp * q_prev)
        local_sum = jnp.sum(packet_now * q_new, axis=(1, 2, 3))
        partials.append(lax.psum(local_sum, "slab") / cells)
        q_prev = q
        q = q_new
    intersections = jnp.stack(partials, axis=0)
    return (q, q_prev, intersections)


def solution(mesh):
    return jax.shard_map(
        shards,
        mesh=mesh,
        in_specs=(
            P("ka", "slab", None, None),
            P("ka", "slab", None, None),
            P("slab", None, None),
            P(),
            P(),
            P(),
            P("slab"),
            P("slab"),
            P(),
        ),
        out_specs=(P("ka", "slab", None, None), P("ka", "slab", None, None), P(None, "ka")),
        check_vma=False,
    )
```

profile of v0, /device:TPU:0, one launch (start us, length us, event | category | flops | bytes accessed | tf_op | source)
XLA Modules:
  0.0 420.4 jit_solution(10612199767086044564)
XLA Ops:
  0.6 0.0 copy-start
  0.6 3.8 copy.81
  4.4 0.0 copy-start.2
  4.4 79.6 %all_to_all.72 = f32[8,256,384]{2,0,1:T(8,128)S(1)} all-to-all(f32[8,256,384]{2,0,1:T(8,128)S(1)} %copy.81), channel_id=1, replica_groups=mesh['ka'=2,'slab'=16] {'slab'}, dimensions={1} | all-to-all | bytes 6291456 | tf_op jit(solution)/shard_map/all_to_all | solution.py:45
  84.0 0.0 copy-done.2
  84.0 2.9 fusion.10
  86.9 3.5 copy.84
  90.4 4.5 %all-to-all-start.1 = ((f32[128,16,384]{2,1,0:T(8,128)}), f32[128,16,384]{2,1,0:T(8,128)}, u32[]{:S(2)}, u32[]{:S(2)}) async-start(f32[128,16,384]{2,1,0:T(8,128)} %copy.84), calls=%async_computation.1 | async-start | bytes 6291456 | tf_op jit(solution)/shard_map/all_to_all | solution.py:47
  94.9 3.5 copy.80
  98.5 1.3 collective-permute-start
  99.7 6.4 %collective-permute-start.1 = (f32[1,8,256,384]{2,3,1,0:T(8,128)}, f32[1,8,256,384]{2,3,1,0:T(8,128)}, u32[]{:S(2)}, u32[]{:S(2)}) collective-permute-start(f32[1,8,256,384]{2,3,1,0:T(8,128)} %copy.80), channel_id=1, source_target_pairs={{0,16},{1,17},{2,18},{3,19},{4,20},{5,21},{6,22},{7,23},{8,24},{9,... | collective-permute-start | bytes 9437192 | tf_op jit(solution)/shard_map/ppermute | solution.py:23
  106.2 3.5 copy.89
  109.8 0.0 copy-start.5
  109.8 0.0 copy-start.4
  109.8 0.0 copy-start.1
  109.8 3.6 copy.92
  113.3 0.0 copy-done.5
  113.3 0.0 copy-done.4
  113.4 0.1 broadcast_multiply_fusion
  113.4 0.0 copy-done.1
  113.4 8.6 %fusion.22 = f32[8,384,256]{2,1,0:T(8,128)} fusion(f32[256,256]{1,0:T(8,128)S(1)} %copy-done.1, f32[1,8,256,384]{3,2,1,0:T(8,128)} %param.10), kind=kOutput, calls=%fused_computation.29 | convolution fusion | flops 2415919104 | bytes 6553600 | tf_op jit(solution)/shard_map/ts,rsp->rtp/dot_general | solution.py:48
  122.0 33.1 %all-to-all-done.1 = f32[128,16,384]{2,1,0:T(8,128)} async-done(((f32[128,16,384]{2,1,0:T(8,128)}), f32[128,16,384]{2,1,0:T(8,128)}, u32[]{:S(2)}, u32[]{:S(2)}) %all-to-all-start.1) | async-done | bytes 3145760 | tf_op jit(solution)/shard_map/all_to_all | solution.py:47
  155.1 3.9 copy.85
  158.9 3.6 copy.86
  162.5 0.0 collective-permute-done
  162.5 0.0 collective-permute-done.1
  162.5 0.0 copy-done
  162.5 0.0 copy-done.3
  162.5 16.2 %fusion.5 = f32[1,8,256,384]{2,3,1,0:T(8,128)} fusion(f32[8,256,384]{1,2,0:T(8,128)} %copy.86, f32[8,384,256]{2,1,0:T(8,128)} %fusion.22, f32[1,8,256,384]{2,3,1,0:T(8,128)} %copy.80, f32[1,8,256,384]{2,3,1,0:T(8,128)} %copy.92, f32[1,8,256,384]{2,3,1,0:T(8,128)} %collective-permute-done.1, f32[1,8,256,384]{2,3,1,0:T(8,128)} %collective-permute-done, ...), kind=kOutput, calls=%fused_computation.9 | convolution fusion | flops 3634888704 | bytes 28909640 | tf_op jit(solution)/shard_map/dot_general | solution.py:50
  178.7 3.6 copy.93
  182.3 84.8 %all_to_all.73 = f32[8,256,384]{2,0,1:T(8,128)S(1)} all-to-all(f32[8,256,384]{2,0,1:T(8,128)} %copy.93), channel_id=1, replica_groups=mesh['ka'=2,'slab'=16] {'slab'}, dimensions={1} | all-to-all | bytes 6291456 | tf_op jit(solution)/shard_map/all_to_all | solution.py:45
  267.0 0.5 copy.95
  267.6 7.1 %fusion.15 = f32[128,16,384]{0,2,1:T(8,128)} fusion(f32[128,16,384]{2,1,0:T(8,128)S(1)} %bitcast.104, f32[128,128]{1,0:T(8,128)S(1)} %copy-done.2), kind=kOutput, calls=%fused_computation.24 | convolution fusion | flops 1207959552 | bytes 6356992 | tf_op jit(solution)/shard_map/sr,rtp->stp/dot_general | solution.py:33
  274.7 3.7 copy.97
  278.4 4.5 %all-to-all-start.3 = ((f32[128,16,384]{2,1,0:T(8,128)}), f32[128,16,384]{2,1,0:T(8,128)}, u32[]{:S(2)}, u32[]{:S(2)}) async-start(f32[128,16,384]{2,1,0:T(8,128)} %copy.97), calls=%async_computation.3 | async-start | bytes 6291456 | tf_op jit(solution)/shard_map/all_to_all | solution.py:47
  282.9 1.3 collective-permute-start.2
  284.2 6.4 %collective-permute-start.3 = (f32[1,8,256,384]{2,3,1,0:T(8,128)}, f32[1,8,256,384]{2,3,1,0:T(8,128)}, u32[]{:S(2)}, u32[]{:S(2)}) collective-permute-start(f32[1,8,256,384]{2,3,1,0:T(8,128)} %fusion.5), channel_id=1, source_target_pairs={{0,16},{1,17},{2,18},{3,19},{4,20},{5,21},{6,22},{7,23},{8,24},{9,... | collective-permute-start | bytes 9437192 | tf_op jit(solution)/shard_map/ppermute | solution.py:23
  290.6 3.5 copy.106
  294.1 6.2 %fusion.20 = f32[8,384,256]{2,1,0:T(8,128)} fusion(f32[256,256]{1,0:T(8,128)S(1)} %copy-done.1, f32[1,8,256,384]{2,3,1,0:T(8,128)} %fusion.5), kind=kOutput, calls=%fused_computation.27 | convolution fusion | flops 2415919104 | bytes 6553600 | tf_op jit(solution)/shard_map/ts,rsp->rtp/dot_general | solution.py:48
  300.3 42.7 %all-to-all-done.3 = f32[128,16,384]{2,1,0:T(8,128)} async-done(((f32[128,16,384]{2,1,0:T(8,128)}), f32[128,16,384]{2,1,0:T(8,128)}, u32[]{:S(2)}, u32[]{:S(2)}) %all-to-all-start.3) | async-done | bytes 3145760 | tf_op jit(solution)/shard_map/all_to_all | solution.py:47
  343.0 3.9 copy.98
  346.9 3.5 copy.99
  350.4 0.0 collective-permute-done.2
  350.4 0.0 collective-permute-done.3
  350.4 15.0 %multiply_reduce_fusion.1 = (f32[]{:T(128)}, f32[]{:T(128)}, f32[1,8,256,384]{2,3,1,0:T(8,128)}) fusion(f32[1,8,256,384]{2,3,1,0:T(8,128)} %copy.80, f32[1,8,256,384]{2,3,1,0:T(8,128)} %fusion.5, f32[1,8,256,384]{2,3,1,0:T(8,128)} %collective-permute-done.3, f32[]{:T(128)S(6)} %div.20, f32[1,8,256,384]{2,3,1,0:T(8,128)} %collective-permute-done.2, ...), kind=kOutput, calls=%fused_computation.23 | convolution fusion | flops 3638034432 | bytes 25763920 | tf_op jit(solution)/shard_map/dot_general | solution.py:50
  365.4 49.6 %all-reduce = (f32[1]{0:T(128)}, f32[1]{0:T(128)}) all-reduce(f32[1]{0:T(128)} %bitcast.30, f32[1]{0:T(128)} %bitcast.28), channel_id=1, replica_groups=mesh['ka'=2,'slab'=16] {'slab'}, use_global_device_ids=true, to_apply=%region_3.0 | all-reduce | flops 2 | bytes 16 | tf_op jit(solution)/shard_map/psum | solution.py:71
  416.3 3.5 copy.105
  419.9 0.6 pad_maximum_fusion
  (2 shorter events, 0.0 us)
Async XLA Ops:
  0.6 161.9 %copy-start = (f32[384,384]{1,0:T(8,128)S(1)}, f32[384,384]{1,0:T(8,128)}, u32[]{:S(2)}) copy-start(f32[384,384]{1,0:T(8,128)} %param.14) | copy-start | bytes 1769476
  4.4 79.6 %copy-start.2 = (f32[128,128]{1,0:T(8,128)S(1)}, f32[128,128]{1,0:T(8,128)}, u32[]{:S(2)}) copy-start(f32[128,128]{1,0:T(8,128)} %param.12) | copy-start | bytes 196612
  90.4 64.7 %all-to-all-start.1 = ((f32[128,16,384]{2,1,0:T(8,128)}), f32[128,16,384]{2,1,0:T(8,128)}, u32[]{:S(2)}, u32[]{:S(2)}) async-start(f32[128,16,384]{2,1,0:T(8,128)} %copy.84), calls=%async_computation.1 | async-start | bytes 6291456 | tf_op jit(solution)/shard_map/all_to_all | solution.py:47
  98.5 64.1 %collective-permute-start = (f32[1,8,256,384]{2,3,1,0:T(8,128)}, f32[1,8,256,384]{2,3,1,0:T(8,128)}, u32[]{:S(2)}, u32[]{:S(2)}) collective-permute-start(f32[1,8,256,384]{2,3,1,0:T(8,128)} %copy.80), channel_id=1, source_target_pairs={{16,0},{17,1},{18,2},{19,3},{20,4},{21,5},{22,6},{23,7},{24,8},{25... | collective-permute-start | bytes 9437192 | tf_op jit(solution)/shard_map/ppermute | solution.py:25
  99.7 62.8 %collective-permute-start.1 = (f32[1,8,256,384]{2,3,1,0:T(8,128)}, f32[1,8,256,384]{2,3,1,0:T(8,128)}, u32[]{:S(2)}, u32[]{:S(2)}) collective-permute-start(f32[1,8,256,384]{2,3,1,0:T(8,128)} %copy.80), channel_id=1, source_target_pairs={{0,16},{1,17},{2,18},{3,19},{4,20},{5,21},{6,22},{7,23},{8,24},{9,... | collective-permute-start | bytes 9437192 | tf_op jit(solution)/shard_map/ppermute | solution.py:23
  109.8 3.6 copy-start.5
  109.8 3.6 copy-start.4
  109.8 3.7 copy-start.1
  158.9 3.6 copy-start.3
  278.4 64.6 %all-to-all-start.3 = ((f32[128,16,384]{2,1,0:T(8,128)}), f32[128,16,384]{2,1,0:T(8,128)}, u32[]{:S(2)}, u32[]{:S(2)}) async-start(f32[128,16,384]{2,1,0:T(8,128)} %copy.97), calls=%async_computation.3 | async-start | bytes 6291456 | tf_op jit(solution)/shard_map/all_to_all | solution.py:47
  282.9 67.5 %collective-permute-start.2 = (f32[1,8,256,384]{2,3,1,0:T(8,128)}, f32[1,8,256,384]{2,3,1,0:T(8,128)}, u32[]{:S(2)}, u32[]{:S(2)}) collective-permute-start(f32[1,8,256,384]{2,3,1,0:T(8,128)} %fusion.5), channel_id=1, source_target_pairs={{16,0},{17,1},{18,2},{19,3},{20,4},{21,5},{22,6},{23,7},{24,8},{25... | collective-permute-start | bytes 9437192 | tf_op jit(solution)/shard_map/ppermute | solution.py:25
  284.2 66.2 %collective-permute-start.3 = (f32[1,8,256,384]{2,3,1,0:T(8,128)}, f32[1,8,256,384]{2,3,1,0:T(8,128)}, u32[]{:S(2)}, u32[]{:S(2)}) collective-permute-start(f32[1,8,256,384]{2,3,1,0:T(8,128)} %fusion.5), channel_id=1, source_target_pairs={{0,16},{1,17},{2,18},{3,19},{4,20},{5,21},{6,22},{7,23},{8,24},{9,... | collective-permute-start | bytes 9437192 | tf_op jit(solution)/shard_map/ppermute | solution.py:23
where the time goes:
time: 421 us; the launch traced here: 420 us
  blocking collectives  214 us (51%)
  waiting for transfers between devices  75.8 us (18%)
  matrix products  56 us (13%)
  local copies, waits for them, and re-layouts  47.6 us (11%)
  starting transfers between devices  24.3 us (6%)
    all_to_all x2, blocking collectives, apply_h(): lax.all_to_all(field, 'slab', split_axis=1, concat_axis=0, tiled=True)  164 us
    all_to_all x2, waiting for transfers between devices, apply_h(): lax.all_to_all(term, 'slab', split_axis=0, concat_axis=1, tiled=True)  75.8 us
    psum x1, blocking collectives, shards(): partials.append(lax.psum(local_sum, 'slab') / cells)  49.6 us
    dot_general x2, matrix products, apply_h(): jnp.dot(field.reshape(rows, field.shape[2]), kin_phi, precision=HI)  31.2 us
    unnamed x17, local copies, waits for them, and re-layouts  17.8 us
    all_to_all x4, local copies, waits for them, and re-layouts, apply_h(): lax.all_to_all(term, 'slab', split_axis=0, concat_axis=1, tiled=True)  14.8 us
    dot_general x2, matrix products, apply_h(): theta_part = jnp.einsum('ts,rsp->rtp', kin_theta, field, precision=HI)  14.8 us
    ppermute x2, starting transfers between devices, padded(): lax.ppermute(tail, axis, [(i, (i + 1) % count) for i in range(ends)])  12.8 us
  transfers between devices with their start and end apart: 6, of which 2 were waited for; matrix products, arithmetic and copies ran while one was open for 10% of the time, Pallas kernels for 0%

commit v1 on v0

--- a/solution.py
+++ b/solution.py
@@ -42,7 +42,13 @@
     near = padded(q, (("ka", 0),), 1)
     field = q[0]
     term = rho_apply(
-        kin_rho, lax.all_to_all(field, "slab", split_axis=1, concat_axis=0, tiled=True)
+        kin_rho,
+        jnp.concatenate(
+            lax.all_to_all(
+                jnp.stack(jnp.split(field, lax.axis_size("slab"), axis=1)), "slab", 0, 0
+            ),
+            axis=0,
+        ),
     )
     rho_part = lax.all_to_all(term, "slab", split_axis=0, concat_axis=1, tiled=True)
     theta_part = jnp.einsum("ts,rsp->rtp", kin_theta, field, precision=HI)

time: 421 us -> 407 us (0.967)
  local copies, waits for them, and re-layouts: 47.6 us -> 24.3 us
  waiting for transfers between devices: 75.8 us -> 91.7 us
  matrix products: 56 us -> 49.3 us
    all_to_all x2, waiting for transfers between devices: 75.8 us -> 91.7 us  [apply_h(): lax.all_to_all(term, 'slab', split_axis=0, concat_axis=1, tiled=True)]
    all_to_all x4 -> x2, local copies, waits for them, and re-layouts: 14.8 us -> 4.67 us  [apply_h(): lax.all_to_all(term, 'slab', split_axis=0, concat_axis=1, tiled=True)]
    dot_general x2, matrix products: 31.2 us -> 22 us  [apply_h(): jnp.dot(field.reshape(rows, field.shape[2]), kin_phi, precision=HI)]
    squeeze x2 -> x0, local copies, waits for them, and re-layouts: 7.36 us -> none  [apply_h(): field = q[0]]
    unnamed x17 -> x54, local copies, waits for them, and re-layouts: 17.8 us -> 12.3 us
  transfers between devices with their start and end apart: 6 -> 6, of which waited for: 2 -> 2; matrix products, arithmetic and copies ran while one was open for 10% -> 4% of each run, Pallas kernels for 0% -> 0%
where the time goes in v1:
time: 407 us; the launch traced here: 406 us
  blocking collectives  214 us (53%)
  waiting for transfers between devices  91.7 us (23%)
  matrix products  49.3 us (12%)
  starting transfers between devices  24.4 us (6%)
  local copies, waits for them, and re-layouts  24.3 us (6%)
    all_to_all x2, blocking collectives, apply_h(): lax.all_to_all(jnp.stack(jnp.split(field, lax.axis_size('slab'), axis=1))...  164 us
    all_to_all x2, waiting for transfers between devices, apply_h(): lax.all_to_all(term, 'slab', split_axis=0, concat_axis=1, tiled=True)  91.7 us
    psum x1, blocking collectives, shards(): partials.append(lax.psum(local_sum, 'slab') / cells)  49.6 us
    dot_general x2, matrix products, apply_h(): jnp.dot(field.reshape(rows, field.shape[2]), kin_phi, precision=HI)  22 us
    dot_general x2, matrix products, rho_apply(): return jnp.einsum('sr,rtp->stp', kin_rho, whole, precision=HI)  14.2 us
    dot_general x2, matrix products, apply_h(): theta_part = jnp.einsum('ts,rsp->rtp', kin_theta, field, precision=HI)  13 us
    ppermute x2, starting transfers between devices, padded(): lax.ppermute(tail, axis, [(i, (i + 1) % count) for i in range(ends)])  12.7 us
    unnamed x54, local copies, waits for them, and re-layouts  12.3 us
  transfers between devices with their start and end apart: 6, of which 2 were waited for; matrix products, arithmetic and copies ran while one was open for 4% of the time, Pallas kernels for 0%

profile of v1, /device:TPU:0, one launch (start us, length us, event | category | flops | bytes accessed | tf_op | source)
XLA Modules:
  0.0 406.4 jit_solution(14143545182470662240)
XLA Ops:
  0.6 0.0 copy-start
  0.6 0.0 copy-start.1
  0.7 1.1 fusion.57
  1.8 1.0 fusion.56
  2.8 0.9 fusion.55
  3.7 0.9 fusion.54
  4.7 0.9 fusion.53
  5.6 0.9 fusion.52
  6.6 0.9 fusion.51
  7.5 0.9 fusion.50
  8.5 0.0 copy-done.1
  8.7 0.0 copy-start.8
  8.7 79.6 %all_to_all.46 = f32[16,8,16,384]{3,2,1,0:T(8,128)S(1)} all-to-all(f32[16,8,16,384]{3,2,1,0:T(8,128)S(1)} %fusion.42), channel_id=1, replica_groups=mesh['ka'=2,'slab'=16] {'slab'}, dimensions={0} | all-to-all | bytes 6291456 | tf_op jit(solution)/shard_map/all_to_all | solution.py:47
  88.2 0.0 copy-done.8
  88.2 7.1 %fusion.14 = f32[128,16,384]{0,2,1:T(8,128)} fusion(f32[128,16,384]{2,1,0:T(8,128)S(1)} %bitcast.249, f32[128,128]{1,0:T(8,128)S(1)} %copy-done.8), kind=kOutput, calls=%fused_computation.22 | convolution fusion | flops 1207959552 | bytes 6356992 | tf_op jit(solution)/shard_map/sr,rtp->stp/dot_general | solution.py:33
  95.4 3.6 copy.27
  98.9 4.6 %all-to-all-start.1 = ((f32[128,16,384]{2,1,0:T(8,128)}), f32[128,16,384]{2,1,0:T(8,128)}, u32[]{:S(2)}, u32[]{:S(2)}) async-start(f32[128,16,384]{2,1,0:T(8,128)} %copy.27), calls=%async_computation.1 | async-start | bytes 6291456 | tf_op jit(solution)/shard_map/all_to_all | solution.py:53
  103.6 1.3 collective-permute-start
  104.9 6.4 %collective-permute-start.1 = (f32[1,8,256,384]{3,2,1,0:T(8,128)}, f32[1,8,256,384]{3,2,1,0:T(8,128)}, u32[]{:S(2)}, u32[]{:S(2)}) collective-permute-start(f32[1,8,256,384]{3,2,1,0:T(8,128)} %param.10), channel_id=1, source_target_pairs={{0,16},{1,17},{2,18},{3,19},{4,20},{5,21},{6,22},{7,23},{8,24},{9,... | collective-permute-start | bytes 9437192 | tf_op jit(solution)/shard_map/ppermute | solution.py:23
  111.4 0.0 copy-done.11
  111.4 0.0 copy-done.10
  111.4 0.1 broadcast_multiply_fusion
  111.5 6.5 %fusion.24 = f32[8,384,256]{1,2,0:T(8,128)} fusion(f32[256,256]{1,0:T(8,128)S(1)} %copy-done.7, f32[1,8,256,384]{3,2,1,0:T(8,128)} %param.10), kind=kOutput, calls=%fused_computation.28 | convolution fusion | flops 2415919104 | bytes 6553600 | tf_op jit(solution)/shard_map/ts,rsp->rtp/dot_general | solution.py:54
  118.0 45.7 %all-to-all-done.1 = f32[128,16,384]{2,1,0:T(8,128)} async-done(((f32[128,16,384]{2,1,0:T(8,128)}), f32[128,16,384]{2,1,0:T(8,128)}, u32[]{:S(2)}, u32[]{:S(2)}) %all-to-all-start.1) | async-done | bytes 3145760 | tf_op jit(solution)/shard_map/all_to_all | solution.py:53
  163.8 2.3 copy.28
  166.1 0.0 collective-permute-done
  166.1 0.0 collective-permute-done.1
  166.1 0.5 copy-done.2
  166.6 1.0 copy-done.6
  167.5 9.9 %fusion.5 = f32[1,8,256,384]{3,2,1,0:T(8,128)S(1)} fusion(f32[8,384,256]{1,2,0:T(8,128)} %fusion.24, f32[8,16,16,384]{3,2,1,0:T(8,128)S(1)} %copy.28, f32[1,8,256,384]{3,2,1,0:T(8,128)} %param.9, f32[1,8,256,384]{3,2,1,0:T(8,128)} %collective-permute-done.1, f32[1,8,256,384]{3,2,1,0:T(8,128)} %collective-permute-done, f32[8,256,384]{2,1,0:T(8,128)S(1)} %copy-done.6, ...), kind=kOutput, calls=%fused_computation.9 | convolution fusion | flops 3634888704 | bytes 25763912 | tf_op jit(solution)/shard_map/dot_general | solution.py:56
  177.4 0.0 copy-start.4
  177.8 1.3 copy-done.4
  179.1 84.5 %all_to_all.47 = f32[16,8,16,384]{3,2,1,0:T(8,128)S(1)} all-to-all(f32[16,8,16,384]{3,2,1,0:T(8,128)S(1)} %fusion.26), channel_id=1, replica_groups=mesh['ka'=2,'slab'=16] {'slab'}, dimensions={0} | all-to-all | bytes 6291456 | tf_op jit(solution)/shard_map/all_to_all | solution.py:47
  263.6 7.1 %fusion.17 = f32[128,16,384]{0,2,1:T(8,128)} fusion(f32[128,16,384]{2,1,0:T(8,128)S(1)} %bitcast.250, f32[128,128]{1,0:T(8,128)S(1)} %copy-done.8), kind=kOutput, calls=%fused_computation.23 | convolution fusion | flops 1207959552 | bytes 6356992 | tf_op jit(solution)/shard_map/sr,rtp->stp/dot_general | solution.py:33
  270.7 3.7 copy.30
  274.4 4.5 %all-to-all-start.3 = ((f32[128,16,384]{2,1,0:T(8,128)}), f32[128,16,384]{2,1,0:T(8,128)}, u32[]{:S(2)}, u32[]{:S(2)}) async-start(f32[128,16,384]{2,1,0:T(8,128)} %copy.30), calls=%async_computation.3 | async-start | bytes 6291456 | tf_op jit(solution)/shard_map/all_to_all | solution.py:53
  278.9 1.3 collective-permute-start.2
  280.2 6.3 %collective-permute-start.3 = (f32[1,8,256,384]{3,2,1,0:T(8,128)}, f32[1,8,256,384]{3,2,1,0:T(8,128)}, u32[]{:S(2)}, u32[]{:S(2)}) collective-permute-start(f32[1,8,256,384]{3,2,1,0:T(8,128)} %copy-done.4), channel_id=1, source_target_pairs={{0,16},{1,17},{2,18},{3,19},{4,20},{5,21},{6,22},{7,23},{8,24},{9,... | collective-permute-start | bytes 9437192 | tf_op jit(solution)/shard_map/ppermute | solution.py:23
  286.6 6.5 %fusion.22 = f32[8,384,256]{1,2,0:T(8,128)} fusion(f32[256,256]{1,0:T(8,128)S(1)} %copy-done.7, f32[1,8,256,384]{3,2,1,0:T(8,128)} %copy-done.4), kind=kOutput, calls=%fused_computation.26 | convolution fusion | flops 2415919104 | bytes 6553600 | tf_op jit(solution)/shard_map/ts,rsp->rtp/dot_general | solution.py:54
  293.1 46.0 %all-to-all-done.3 = f32[128,16,384]{2,1,0:T(8,128)} async-done(((f32[128,16,384]{2,1,0:T(8,128)}), f32[128,16,384]{2,1,0:T(8,128)}, u32[]{:S(2)}, u32[]{:S(2)}) %all-to-all-start.3) | async-done | bytes 3145760 | tf_op jit(solution)/shard_map/all_to_all | solution.py:53
  339.0 2.3 copy.31
  341.4 0.0 collective-permute-done.2
  341.4 0.0 collective-permute-done.3
  341.4 0.5 copy-done.3
  341.9 1.0 copy-done.5
  342.8 12.1 %multiply_reduce_fusion.1 = (f32[]{:T(128)}, f32[]{:T(128)}, f32[1,8,256,384]{3,2,1,0:T(8,128)}) fusion(f32[1,8,256,384]{3,2,1,0:T(8,128)S(1)} %copy-done.3, f32[1,8,256,384]{3,2,1,0:T(8,128)S(1)} %copy-done.5, f32[1,8,256,384]{3,2,1,0:T(8,128)} %collective-permute-done.3, f32[]{:T(128)S(6)} %div.20, f32[1,8,256,384]{3,2,1,0:T(8,128)} %collective-permute-done.2, ...), kind=kOutput, calls=%fused_computation.21 | convolution fusion | flops 3638034432 | bytes 25763920 | tf_op jit(solution)/shard_map/dot_general | solution.py:56
  355.0 49.6 %all-reduce = (f32[1]{0:T(128)}, f32[1]{0:T(128)}) all-reduce(f32[1]{0:T(128)} %bitcast.55, f32[1]{0:T(128)} %bitcast.53), channel_id=1, replica_groups=mesh['ka'=2,'slab'=16] {'slab'}, use_global_device_ids=true, to_apply=%region_3.0 | all-reduce | flops 2 | bytes 16 | tf_op jit(solution)/shard_map/psum | solution.py:77
  405.8 0.6 pad_maximum_fusion
  (36 shorter events, 0.4 us)
Async XLA Ops:
  0.6 165.5 %copy-start = (f32[384,384]{1,0:T(8,128)S(1)}, f32[384,384]{1,0:T(8,128)}, u32[]{:S(2)}) copy-start(f32[384,384]{1,0:T(8,128)} %param.14) | copy-start | bytes 1769476
  0.6 7.8 %copy-start.1 = (f32[1,8,256,384]{3,2,1,0:T(8,128)S(1)}, f32[1,8,256,384]{3,2,1,0:T(8,128)}, u32[]{:S(2)}) copy-start(f32[1,8,256,384]{3,2,1,0:T(8,128)} %param.10) | copy-start | bytes 9437188
  8.7 79.6 %copy-start.8 = (f32[128,128]{1,0:T(8,128)S(1)}, f32[128,128]{1,0:T(8,128)}, u32[]{:S(2)}) copy-start(f32[128,128]{1,0:T(8,128)} %param.12) | copy-start | bytes 196612
  98.9 12.5 %copy-start.11 = (f32[8]{0:T(128)S(1)}, f32[8]{0:T(128)}, u32[]{:S(2)}) copy-start(f32[8]{0:T(128)} %param.16) | copy-start | bytes 100
  98.9 12.5 %copy-start.10 = (f32[256]{0:T(256)S(1)}, f32[256]{0:T(256)}, u32[]{:S(2)}) copy-start(f32[256]{0:T(256)} %param.17) | copy-start | bytes 3076
  98.9 12.6 %copy-start.7 = (f32[256,256]{1,0:T(8,128)S(1)}, f32[256,256]{1,0:T(8,128)}, u32[]{:S(2)}) copy-start(f32[256,256]{1,0:T(8,128)} %param.13) | copy-start | bytes 786436
  98.9 64.8 %all-to-all-start.1 = ((f32[128,16,384]{2,1,0:T(8,128)}), f32[128,16,384]{2,1,0:T(8,128)}, u32[]{:S(2)}, u32[]{:S(2)}) async-start(f32[128,16,384]{2,1,0:T(8,128)} %copy.27), calls=%async_computation.1 | async-start | bytes 6291456 | tf_op jit(solution)/shard_map/all_to_all | solution.py:53
  103.6 62.5 %collective-permute-start = (f32[1,8,256,384]{3,2,1,0:T(8,128)}, f32[1,8,256,384]{3,2,1,0:T(8,128)}, u32[]{:S(2)}, u32[]{:S(2)}) collective-permute-start(f32[1,8,256,384]{3,2,1,0:T(8,128)} %param.10), channel_id=1, source_target_pairs={{16,0},{17,1},{18,2},{19,3},{20,4},{21,5},{22,6},{23,7},{24,8},{25... | collective-permute-start | bytes 9437192 | tf_op jit(solution)/shard_map/ppermute | solution.py:25
  104.9 61.2 %collective-permute-start.1 = (f32[1,8,256,384]{3,2,1,0:T(8,128)}, f32[1,8,256,384]{3,2,1,0:T(8,128)}, u32[]{:S(2)}, u32[]{:S(2)}) collective-permute-start(f32[1,8,256,384]{3,2,1,0:T(8,128)} %param.10), channel_id=1, source_target_pairs={{0,16},{1,17},{2,18},{3,19},{4,20},{5,21},{6,22},{7,23},{8,24},{9,... | collective-permute-start | bytes 9437192 | tf_op jit(solution)/shard_map/ppermute | solution.py:23
  111.5 54.6 %copy-start.9 = (f32[8]{0:T(128)S(1)}, f32[8]{0:T(128)}, u32[]{:S(2)}) copy-start(f32[8]{0:T(128)} %param.15) | copy-start | bytes 100
  163.7 2.8 copy-start.2
  163.8 3.8 copy-start.6
  177.4 1.7 copy-start.4
  274.4 64.6 %all-to-all-start.3 = ((f32[128,16,384]{2,1,0:T(8,128)}), f32[128,16,384]{2,1,0:T(8,128)}, u32[]{:S(2)}, u32[]{:S(2)}) async-start(f32[128,16,384]{2,1,0:T(8,128)} %copy.30), calls=%async_computation.3 | async-start | bytes 6291456 | tf_op jit(solution)/shard_map/all_to_all | solution.py:53
  278.9 62.5 %collective-permute-start.2 = (f32[1,8,256,384]{3,2,1,0:T(8,128)}, f32[1,8,256,384]{3,2,1,0:T(8,128)}, u32[]{:S(2)}, u32[]{:S(2)}) collective-permute-start(f32[1,8,256,384]{3,2,1,0:T(8,128)} %copy-done.4), channel_id=1, source_target_pairs={{16,0},{17,1},{18,2},{19,3},{20,4},{21,5},{22,6},{23,7},{24,8},{25... | collective-permute-start | bytes 9437192 | tf_op jit(solution)/shard_map/ppermute | solution.py:25
  280.2 61.2 %collective-permute-start.3 = (f32[1,8,256,384]{3,2,1,0:T(8,128)}, f32[1,8,256,384]{3,2,1,0:T(8,128)}, u32[]{:S(2)}, u32[]{:S(2)}) collective-permute-start(f32[1,8,256,384]{3,2,1,0:T(8,128)} %copy-done.4), channel_id=1, source_target_pairs={{0,16},{1,17},{2,18},{3,19},{4,20},{5,21},{6,22},{7,23},{8,24},{9,... | collective-permute-start | bytes 9437192 | tf_op jit(solution)/shard_map/ppermute | solution.py:23
  339.0 2.8 copy-start.3
  339.0 3.8 copy-start.5
